TPU v7x, 32 devices: a whole 2x2x4 slice. The times are simulated.
32 devices in a mesh: dp: 16 (over z, y, core), tensor: 2 (over x).
Axes of the slice: x: 2, y: 2, z: 4, core: 2. Of those that a mesh axis runs over, the one named last changes fastest.
Arguments:
- tokens: bfloat16 [32768, 1024], P(('dp', 'tensor')), may hold values from -12 to 12
- query_matrix: bfloat16 [1024, 1024], P(None, 'tensor'), may hold values from -0.1875 to 0.1875
- key_weight: bfloat16 [1024, 1024], P(None, 'tensor'), may hold values from -0.1875 to 0.1875
- value_weight: bfloat16 [1024, 1024], P(None, 'tensor'), may hold values from -0.1875 to 0.1875
- gate_weight: bfloat16 [1024, 1024], P(None, 'tensor'), may hold values from -0.1875 to 0.1875
- out_weight: bfloat16 [1024, 1024], P('tensor'), may hold values from -0.1875 to 0.1875
- left_weight: bfloat16 [1024, 2816], P(None, 'tensor'), may hold values from -0.1875 to 0.1875
- right_weight: bfloat16 [1024, 2816], P(None, 'tensor'), may hold values from -0.1875 to 0.1875
- down_weight: bfloat16 [2816, 1024], P('tensor'), may hold values from -0.109375 to 0.109375
- cotangent: bfloat16 [32768, 1024], P(('dp', 'tensor')), may hold values from -6 to 6
Outputs:
- result: bfloat16 [32768, 1024], P(('dp', 'tensor'))
- tokens_grad: float32 [32768, 1024], P(('dp', 'tensor'))
- query_weight_grad: float32 [1024, 1024], P('dp', 'tensor')
- key_weight_grad: float32 [1024, 1024], P('dp', 'tensor')
- value_weight_grad: float32 [1024, 1024], P('dp', 'tensor')
- gate_matrix_gradient: float32 [1024, 1024], P('dp', 'tensor')
- out_weight_grad: float32 [1024, 1024], P('tensor', 'dp')
- left_weight_grad: float32 [1024, 2816], P('dp', 'tensor')
- right_weight_grad: float32 [1024, 2816], P('dp', 'tensor')
- down_weight_grad: float32 [2816, 1024], P('tensor', 'dp')
All inputs are finite; a program needn't handle non-finite values.
Results may differ from a plain program's by a relative error of at most 0.015.
Values may be sent and summed in bfloat16 or wider, within the bound.
No kernel may reach another device: no remote copies, remote signals or barrier semaphores. Data moves between devices by JAX's collectives and lax.ppermute only.
A program may use at most 256 MiB of HBM per device.

v0:
```python
import jax
import jax.numpy as jnp
from jax import lax
from jax.sharding import PartitionSpec as P

HEADS = 16
HEAD_DIM = 64
SEQ_LEN = 2048
BLOCK = 512


EPS = 1e-06


def norm_rows(values):
    factor = lax.rsqrt(jnp.mean(values * values, axis=-1, keepdims=True) + EPS)
    return (values * factor, factor)


def norm_back(grad_rows, normed, factor):
    return factor * (grad_rows - normed * jnp.mean(grad_rows * normed, axis=-1, keepdims=True))


def causal_mask():
    row_ids = lax.broadcasted_iota(jnp.int32, (BLOCK, BLOCK), 0)
    col_ids = lax.broadcasted_iota(jnp.int32, (BLOCK, BLOCK), 1)
    return (row_ids >= col_ids).astype(jnp.float32)


def to_blocks(values, local_heads):
    seq_count = values.shape[0] // SEQ_LEN
    shaped = values.reshape(seq_count, SEQ_LEN // BLOCK, BLOCK, local_heads, HEAD_DIM)
    return jnp.moveaxis(shaped, 1, 0)


def from_blocks(pieces):
    moved = jnp.moveaxis(pieces, 0, 1)
    return moved.reshape(moved.shape[0] * SEQ_LEN, -1)


def attend_forward(query_rows, key_rows, value_rows, local_heads):
    causal = causal_mask()

    def step_fn(running_state, pieces):
        query_part, key_portion, value_portion = pieces
        scores = jnp.einsum(
            "sqhe,skhe->shqk", query_part, key_portion, preferred_element_type=jnp.float32
        )
        weights_low = (scores * causal).astype(jnp.bfloat16)
        inside = jnp.einsum(
            "shqk,skhe->sqhe", weights_low, value_portion, preferred_element_type=jnp.float32
        )
        carried = jnp.einsum(
            "sqhe,shef->sqhf",
            query_part.astype(jnp.float32),
            running_state,
            precision=lax.Precision.HIGHEST,
        )
        following_state = running_state + jnp.einsum(
            "skhe,skhf->shef", key_portion, value_portion, preferred_element_type=jnp.float32
        )
        return (following_state, (inside + carried, running_state))

    seq_count = query_rows.shape[0] // SEQ_LEN
    start_state = jnp.zeros((seq_count, local_heads, HEAD_DIM, HEAD_DIM), jnp.float32)
    pieces = (
        to_blocks(query_rows, local_heads),
        to_blocks(key_rows, local_heads),
        to_blocks(value_rows, local_heads),
    )
    _, (outputs, states) = lax.scan(step_fn, start_state, pieces)
    return (from_blocks(outputs), states)


def attend_backward(query_rows, key_rows, value_rows, grad_rows, states, local_heads):
    causal = causal_mask()

    def step_fn(later_sum, pieces):
        query_part, key_portion, value_portion, grad_part, running_state = pieces
        scores = jnp.einsum(
            "sqhe,skhe->shqk", query_part, key_portion, preferred_element_type=jnp.float32
        )
        weights_low = (scores * causal).astype(jnp.bfloat16)
        raw_grad = jnp.einsum(
            "sqhe,skhe->shqk", grad_part, value_portion, preferred_element_type=jnp.float32
        )
        prob_grad = (raw_grad * causal).astype(jnp.bfloat16)
        query_grad = jnp.einsum(
            "shqk,skhe->sqhe", prob_grad, key_portion, preferred_element_type=jnp.float32
        )
        query_grad = query_grad + jnp.einsum(
            "sqhf,shef->sqhe",
            grad_part.astype(jnp.float32),
            running_state,
            precision=lax.Precision.HIGHEST,
        )
        key_grad = jnp.einsum(
            "shqk,sqhe->skhe", prob_grad, query_part, preferred_element_type=jnp.float32
        )
        key_grad = key_grad + jnp.einsum(
            "skhf,shef->skhe",
            value_portion.astype(jnp.float32),
            later_sum,
            precision=lax.Precision.HIGHEST,
        )
        value_grad = jnp.einsum(
            "shqk,sqhe->skhe", weights_low, grad_part, preferred_element_type=jnp.float32
        )
        value_grad = value_grad + jnp.einsum(
            "skhe,shef->skhf",
            key_portion.astype(jnp.float32),
            later_sum,
            precision=lax.Precision.HIGHEST,
        )
        earlier = later_sum + jnp.einsum(
            "sqhe,sqhf->shef", query_part, grad_part, preferred_element_type=jnp.float32
        )
        return (earlier, (query_grad, key_grad, value_grad))

    seq_count = query_rows.shape[0] // SEQ_LEN
    start_sum = jnp.zeros((seq_count, local_heads, HEAD_DIM, HEAD_DIM), jnp.float32)
    pieces = (
        to_blocks(query_rows, local_heads),
        to_blocks(key_rows, local_heads),
        to_blocks(value_rows, local_heads),
        to_blocks(grad_rows, local_heads),
        states,
    )
    _, (query_grads, key_grads, value_grads) = lax.scan(step_fn, start_sum, pieces, reverse=True)
    return (from_blocks(query_grads), from_blocks(key_grads), from_blocks(value_grads))


def body(
    tokens,
    query_matrix,
    key_weight,
    value_weight,
    gate_weight,
    out_weight,
    left_weight,
    right_weight,
    down_weight,
    cotangent,
):
    local_heads = HEADS // lax.axis_size("tensor")
    inputs = tokens.astype(jnp.float32)
    normed_in, norm_in = norm_rows(inputs)
    normed_low = normed_in.astype(jnp.bfloat16)
    normed_all = lax.all_gather(normed_low, "tensor", axis=0, tiled=True)
    all_rows = normed_all.shape[0]
    query_pre = jnp.dot(normed_all, query_matrix, preferred_element_type=jnp.float32)
    key_pre = jnp.dot(normed_all, key_weight, preferred_element_type=jnp.float32)
    query_rows = jax.nn.softplus(query_pre).astype(jnp.bfloat16)
    key_rows = jax.nn.softplus(key_pre).astype(jnp.bfloat16)
    value_rows = jnp.dot(normed_all, value_weight, preferred_element_type=jnp.float32).astype(
        jnp.bfloat16
    )
    gate_pre = jnp.dot(normed_all, gate_weight, preferred_element_type=jnp.float32)
    attn, states = attend_forward(query_rows, key_rows, value_rows, local_heads)
    heads_view = attn.reshape(all_rows, local_heads, HEAD_DIM)
    mean_square = jnp.mean(heads_view * heads_view, axis=-1, keepdims=True)
    head_factor = lax.rsqrt(jnp.maximum(mean_square, 1.0))
    above_floor = (mean_square > 1.0).astype(jnp.float32)
    normed_heads = heads_view * head_factor
    normed_attn = normed_heads.reshape(all_rows, -1)
    mixed_low = (normed_attn * gate_pre).astype(jnp.bfloat16)
    piece = mixed_low
    branch = lax.psum_scatter(
        jnp.dot(piece, out_weight, preferred_element_type=jnp.float32),
        "tensor",
        scatter_dimension=0,
        tiled=True,
    )
    residual = inputs + branch
    normed_mid, norm_mid = norm_rows(residual)
    normed_mid_low = normed_mid.astype(jnp.bfloat16)
    mid_all = lax.all_gather(normed_mid_low, "tensor", axis=0, tiled=True)
    left_act = jnp.dot(mid_all, left_weight, preferred_element_type=jnp.float32)
    right_act = jnp.dot(mid_all, right_weight, preferred_element_type=jnp.float32)
    product_low = (left_act * right_act).astype(jnp.bfloat16)
    piece = product_low
    ffn_out = lax.psum_scatter(
        jnp.dot(piece, down_weight, preferred_element_type=jnp.float32),
        "tensor",
        scatter_dimension=0,
        tiled=True,
    )
    result = residual + ffn_out
    cot_all = lax.all_gather(cotangent, "tensor", axis=0, tiled=True)
    down_grad = jnp.einsum("rf,rd->fd", product_low, cot_all, preferred_element_type=jnp.float32)
    product_grad = jnp.einsum("rd,fd->rf", cot_all, down_weight, preferred_element_type=jnp.float32)
    left_low = (product_grad * right_act).astype(jnp.bfloat16)
    right_low = (product_grad * left_act).astype(jnp.bfloat16)
    mid_back = lax.all_gather(normed_mid_low, "tensor", axis=0, tiled=True)
    left_grad = jnp.einsum("rd,rf->df", mid_back, left_low, preferred_element_type=jnp.float32)
    right_grad = jnp.einsum("rd,rf->df", mid_back, right_low, preferred_element_type=jnp.float32)
    total = jnp.einsum("rf,df->rd", left_low, left_weight, preferred_element_type=jnp.float32)
    mid_grad = lax.psum_scatter(
        total
        + jnp.einsum("rf,df->rd", right_low, right_weight, preferred_element_type=jnp.float32),
        "tensor",
        scatter_dimension=0,
        tiled=True,
    )
    resid_grad = cotangent.astype(jnp.float32) + norm_back(mid_grad, normed_mid, norm_mid)
    resid_low = resid_grad.astype(jnp.bfloat16)
    resid_all = lax.all_gather(resid_low, "tensor", axis=0, tiled=True)
    out_grad = jnp.einsum("rc,rd->cd", mixed_low, resid_all, preferred_element_type=jnp.float32)
    mixed_grad = jnp.einsum("rd,cd->rc", resid_all, out_weight, preferred_element_type=jnp.float32)
    gate_low = (mixed_grad * normed_attn).astype(jnp.bfloat16)
    normed_grad = (mixed_grad * gate_pre).reshape(all_rows, local_heads, HEAD_DIM)
    projection = (
        above_floor * normed_heads * jnp.mean(normed_grad * normed_heads, axis=-1, keepdims=True)
    )
    attn_grad = head_factor * (normed_grad - projection)
    attn_low = attn_grad.reshape(all_rows, -1).astype(jnp.bfloat16)
    query_grad, key_grad, value_grad = attend_backward(
        query_rows, key_rows, value_rows, attn_low, states, local_heads
    )
    query_low = (query_grad * jax.nn.sigmoid(query_pre)).astype(jnp.bfloat16)
    key_low = (key_grad * jax.nn.sigmoid(key_pre)).astype(jnp.bfloat16)
    value_low = value_grad.astype(jnp.bfloat16)
    normed_back = lax.all_gather(normed_low, "tensor", axis=0, tiled=True)
    query_wgrad = jnp.einsum(
        "rd,rc->dc", normed_back, query_low, preferred_element_type=jnp.float32
    )
    key_weight_gradient = jnp.einsum(
        "rd,rc->dc", normed_back, key_low, preferred_element_type=jnp.float32
    )
    value_wgrad = jnp.einsum(
        "rd,rc->dc", normed_back, value_low, preferred_element_type=jnp.float32
    )
    gate_wgrad = jnp.einsum("rd,rc->dc", normed_back, gate_low, preferred_element_type=jnp.float32)
    total = jnp.einsum("rc,dc->rd", query_low, query_matrix, preferred_element_type=jnp.float32)
    total = total + jnp.einsum("rc,dc->rd", key_low, key_weight, preferred_element_type=jnp.float32)
    total = total + jnp.einsum(
        "rc,dc->rd", value_low, value_weight, preferred_element_type=jnp.float32
    )
    in_grad = lax.psum_scatter(
        total + jnp.einsum("rc,dc->rd", gate_low, gate_weight, preferred_element_type=jnp.float32),
        "tensor",
        scatter_dimension=0,
        tiled=True,
    )
    tokens_grad = resid_grad + norm_back(in_grad, normed_in, norm_in)
    summed = (
        lax.psum_scatter(query_wgrad, "dp", scatter_dimension=0, tiled=True),
        lax.psum_scatter(key_weight_gradient, "dp", scatter_dimension=0, tiled=True),
        lax.psum_scatter(value_wgrad, "dp", scatter_dimension=0, tiled=True),
        lax.psum_scatter(gate_wgrad, "dp", scatter_dimension=0, tiled=True),
        lax.psum_scatter(out_grad, "dp", scatter_dimension=1, tiled=True),
        lax.psum_scatter(left_grad, "dp", scatter_dimension=0, tiled=True),
        lax.psum_scatter(right_grad, "dp", scatter_dimension=0, tiled=True),
        lax.psum_scatter(down_grad, "dp", scatter_dimension=1, tiled=True),
    )
    return (
        result.astype(jnp.bfloat16),
        tokens_grad,
        summed[0],
        summed[1],
        summed[2],
        summed[3],
        summed[4],
        summed[5],
        summed[6],
        summed[7],
    )


def solution(mesh):
    placed = (
        P(("dp", "tensor"), None),
        P(None, "tensor"),
        P(None, "tensor"),
        P(None, "tensor"),
        P(None, "tensor"),
        P("tensor", None),
        P(None, "tensor"),
        P(None, "tensor"),
        P("tensor", None),
        P(("dp", "tensor"), None),
    )
    return jax.shard_map(
        body,
        mesh=mesh,
        in_specs=placed,
        out_specs=(
            P(("dp", "tensor"), None),
            P(("dp", "tensor"), None),
            P("dp", "tensor"),
            P("dp", "tensor"),
            P("dp", "tensor"),
            P("dp", "tensor"),
            P("tensor", "dp"),
            P("dp", "tensor"),
            P("dp", "tensor"),
            P("tensor", "dp"),
        ),
        check_vma=False,
    )
```

profile of v0, /device:TPU:0, one launch (start us, length us, event | category | flops | bytes accessed | tf_op | source)
XLA Modules:
  0.0 1622.1 jit_solution(7593486317118650088)
XLA Ops:
  13.5 59.5 %all-gather.5.cloned.1.call-done = bf16[2048,1024]{1,0:T(8,128)(2,1)} async-done(((bf16[1024,1024]{1,0:T(8,128)(2,1)}), bf16[2048,1024]{1,0:T(8,128)(2,1)}) %all-gather.5.cloned.1.call-update) | async-done | bytes 4194320 | tf_op jit(solution)/shard_map/all_gather | solution.py:149
  135.4 46.7 %while.37 = (s32[]{:T(128)}, f32[1,8,64,64]{3,2,1,0:T(8,128)S(1)}, f32[4,1,512,8,64]{2,4,3,1,0:T(8,128)}, f32[4,1,8,64,64]{4,3,2,1,0:T(8,128)}, bf16[4,1,512,8,6...) while((s32[]{:T(128)}, f32[1,8,64,64]{3,2,1,0:T(8,128)S(1)}, ...), condition=%wide.region_2.3_spmd.clone, body=%wide.region_1.2_spmd.clone.sunk | while | flops 776863744 | bytes 9179241 | solution.py:71
  204.9 99.4 %reduce-scatter.13.cloned.1.call-done = f32[1024,1024]{1,0:T(8,128)} async-done(((f32[2048,1024]{1,0:T(8,128)}), f32[1024,1024]{1,0:T(8,128)}) %reduce-scatter.13.cloned.1.call-update) | async-done | bytes 4194320 | tf_op jit(solution)/shard_map/reduce_scatter | solution.py:168
  311.4 56.3 %all-gather.7.cloned.1.call-done = bf16[2048,1024]{1,0:T(8,128)(2,1)} async-done(((bf16[1024,1024]{1,0:T(8,128)(2,1)}), bf16[2048,1024]{1,0:T(8,128)(2,1)}) %all-gather.7.cloned.1.call-update) | async-done | bytes 4194320 | tf_op jit(solution)/shard_map/all_gather | solution.py:177
  367.7 12.1 fusion.117
  389.1 36.8 %all-gather.9.cloned.1.call-done = bf16[2048,1024]{1,0:T(8,128)(2,1)} async-done(((bf16[1024,1024]{1,0:T(8,128)(2,1)}), bf16[2048,1024]{1,0:T(8,128)(2,1)}) %all-gather.9.cloned.1.call-update) | async-done | bytes 4194320 | tf_op jit(solution)/shard_map/all_gather | solution.py:189
  425.9 15.7 multiply_convert_fusion.5
  460.8 99.1 %reduce-scatter.17.cloned.1.call-done = f32[1024,1024]{1,0:T(8,128)} async-done(((f32[2048,1024]{1,0:T(8,128)}), f32[1024,1024]{1,0:T(8,128)}) %reduce-scatter.17.cloned.1.call-update) | async-done | bytes 4194320 | tf_op jit(solution)/shard_map/reduce_scatter | solution.py:198
  578.4 49.2 %all-gather.11.cloned.1.call-done = bf16[2048,1024]{1,0:T(8,128)(2,1)} async-done(((bf16[1024,1024]{1,0:T(8,128)(2,1)}), bf16[2048,1024]{1,0:T(8,128)(2,1)}) %all-gather.11.cloned.1.call-update) | async-done | bytes 4194320 | tf_op jit(solution)/shard_map/all_gather | solution.py:207
  652.3 108.7 %while.38 = (s32[]{:T(128)}, f32[1,8,64,64]{3,2,1,0:T(8,128)S(1)}, f32[4,1,512,8,64]{2,4,3,1,0:T(8,128)}, f32[4,1,512,8,64]{2,4,3,1,0:T(8,128)}, bf16[4,1,512,8,...) while((s32[]{:T(128)}, f32[1,8,64,64]{3,2,1,0:T(8,128)S(1)}, ...), condition=%wide.region_11.12_spmd.clone.clone, body=%wide.region_10.11_spmd.clone.clone.sunk | while | flops 1989541888 | bytes 53224144 | solution.py:129
  819.8 12.6 add_add_fusion
  843.4 11.9 fusion.129
  855.4 11.8 fusion.130
  867.2 11.9 fusion.131
  913.5 18.4 %reduce-scatter.19.cloned.1.call-done = f32[1024,1024]{1,0:T(8,128)} async-done(((f32[2048,1024]{1,0:T(8,128)}), f32[1024,1024]{1,0:T(8,128)}) %reduce-scatter.19.cloned.1.call-update) | async-done | bytes 4194320 | tf_op jit(solution)/shard_map/reduce_scatter | solution.py:239
  935.4 98.1 %reduce-scatter.15.cloned.1.call-done = f32[1024,1024]{1,0:T(8,128)} async-done(((f32[2048,1024]{1,0:T(8,128)}), f32[1024,1024]{1,0:T(8,128)}) %reduce-scatter.15.cloned.1.call-update) | async-done | bytes 4194320 | tf_op jit(solution)/shard_map/reduce_scatter | solution.py:182
  1044.7 74.9 %reduce-scatter.31.cloned.1.call-done = f32[64,1408]{1,0:T(8,128)} async-done(((f32[1024,1408]{1,0:T(8,128)}), f32[64,1408]{1,0:T(8,128)}) %reduce-scatter.31.cloned.1.call-update) | async-done | bytes 360464 | tf_op jit(solution)/shard_map/reduce_scatter | solution.py:252
  1119.6 85.1 %reduce-scatter.33.cloned.1.call-done = f32[64,1408]{1,0:T(8,128)} async-done(((f32[1024,1408]{1,0:T(8,128)}), f32[64,1408]{1,0:T(8,128)}) %reduce-scatter.33.cloned.1.call-update) | async-done | bytes 360464 | tf_op jit(solution)/shard_map/reduce_scatter | solution.py:253
  1204.7 85.2 %reduce-scatter.35.cloned.1.call-done = f32[1408,64]{0,1:T(8,128)} async-done(((f32[1408,1024]{0,1:T(8,128)}), f32[1408,64]{0,1:T(8,128)}) %reduce-scatter.35.cloned.1.call-update) | async-done | bytes 360464 | tf_op jit(solution)/shard_map/reduce_scatter | solution.py:254
  1289.9 65.0 %reduce-scatter.29.cloned.1.call-done = f32[512,64]{0,1:T(8,128)} async-done(((f32[512,1024]{0,1:T(8,128)}), f32[512,64]{0,1:T(8,128)}) %reduce-scatter.29.cloned.1.call-update) | async-done | bytes 131088 | tf_op jit(solution)/shard_map/reduce_scatter | solution.py:251
  1354.9 65.4 %reduce-scatter.21.cloned.1.call-done = f32[64,512]{1,0:T(8,128)} async-done(((f32[1024,512]{1,0:T(8,128)}), f32[64,512]{1,0:T(8,128)}) %reduce-scatter.21.cloned.1.call-update) | async-done | bytes 131088 | tf_op jit(solution)/shard_map/reduce_scatter | solution.py:247
  1420.3 64.8 %reduce-scatter.23.cloned.1.call-done = f32[64,512]{1,0:T(8,128)} async-done(((f32[1024,512]{1,0:T(8,128)}), f32[64,512]{1,0:T(8,128)}) %reduce-scatter.23.cloned.1.call-update) | async-done | bytes 131088 | tf_op jit(solution)/shard_map/reduce_scatter | solution.py:248
  1485.1 65.2 %reduce-scatter.25.cloned.1.call-done = f32[64,512]{1,0:T(8,128)} async-done(((f32[1024,512]{1,0:T(8,128)}), f32[64,512]{1,0:T(8,128)}) %reduce-scatter.25.cloned.1.call-update) | async-done | bytes 131088 | tf_op jit(solution)/shard_map/reduce_scatter | solution.py:249
  1550.4 64.8 %reduce-scatter.27.cloned.1.call-done = f32[64,512]{1,0:T(8,128)} async-done(((f32[1024,512]{1,0:T(8,128)}), f32[64,512]{1,0:T(8,128)}) %reduce-scatter.27.cloned.1.call-update) | async-done | bytes 131088 | tf_op jit(solution)/shard_map/reduce_scatter | solution.py:250
  (236 shorter events, 443.0 us)
Async XLA Ops:
  7.2 418.8 %copy-start = (bf16[1408,1024]{1,0:T(8,128)(2,1)S(1)}, bf16[1408,1024]{1,0:T(8,128)(2,1)}, u32[]{:S(2)}) copy-start(bf16[1408,1024]{1,0:T(8,128)(2,1)} %param.22) | copy-start | bytes 8650756
  7.2 65.8 %all-gather.5.cloned.1.call-start = ((), (), s32[]{:S(2)}) async-start(), calls=%async_computation.12 | async-start | bytes 6291456 | tf_op jit(solution)/shard_map/all_gather | solution.py:149
  13.4 290.8 %reduce-scatter.13.cloned.1.call-start = ((), (), s32[]{:S(2)}) async-start(), calls=%async_computation.13 | async-start | bytes 12582912 | tf_op jit(solution)/shard_map/reduce_scatter | solution.py:168
  204.8 162.8 %all-gather.7.cloned.1.call-start = ((), (), s32[]{:S(2)}) async-start(), calls=%async_computation.14 | async-start | bytes 6291456 | tf_op jit(solution)/shard_map/all_gather | solution.py:177
  308.9 256.0 %copy-start.23 = (f32[1024]{0:T(1024)}, f32[1024]{0:T(1024)S(1)}, u32[]{:S(2)}) copy-start(f32[1024]{0:T(1024)S(1)} %add_rsqrt_fusion) | copy-start | bytes 12292
  310.8 115.2 %all-gather.9.cloned.1.call-start = ((), (), s32[]{:S(2)}) async-start(), calls=%async_computation.16 | async-start | bytes 6291456 | tf_op jit(solution)/shard_map/all_gather | solution.py:189
  311.4 248.5 %reduce-scatter.17.cloned.1.call-start = ((), (), s32[]{:S(2)}) async-start(), calls=%async_computation.17 | async-start | bytes 12582912 | tf_op jit(solution)/shard_map/reduce_scatter | solution.py:198
  367.7 12.1 copy-start.29
  367.7 12.1 copy-start.30
  441.6 9.8 copy-start.31
  460.5 167.1 %all-gather.11.cloned.1.call-start = ((), (), s32[]{:S(2)}) async-start(), calls=%async_computation.18 | async-start | bytes 6291456 | tf_op jit(solution)/shard_map/all_gather | solution.py:207
  570.7 361.1 %reduce-scatter.19.cloned.1.call-start = ((), (), s32[]{:S(2)}) async-start(), calls=%async_computation.19 | async-start | bytes 12582912 | tf_op jit(solution)/shard_map/reduce_scatter | solution.py:239
  832.4 201.1 %reduce-scatter.15.cloned.1.call-start = ((), (), s32[]{:S(2)}) async-start(), calls=%async_computation.15 | async-start | bytes 12582912 | tf_op jit(solution)/shard_map/reduce_scatter | solution.py:182
  843.4 276.2 %reduce-scatter.31.cloned.1.call-start = ((), (), s32[]{:S(2)}) async-start(), calls=%async_computation.25 | async-start | bytes 6127616 | tf_op jit(solution)/shard_map/reduce_scatter | solution.py:252
  855.3 349.4 %reduce-scatter.33.cloned.1.call-start = ((), (), s32[]{:S(2)}) async-start(), calls=%async_computation.26 | async-start | bytes 6127616 | tf_op jit(solution)/shard_map/reduce_scatter | solution.py:253
  867.2 422.7 %reduce-scatter.35.cloned.1.call-start = ((), (), s32[]{:S(2)}) async-start(), calls=%async_computation.27 | async-start | bytes 6127616 | tf_op jit(solution)/shard_map/reduce_scatter | solution.py:254
  879.2 475.8 %reduce-scatter.29.cloned.1.call-start = ((), (), s32[]{:S(2)}) async-start(), calls=%async_computation.24 | async-start | bytes 2228224 | tf_op jit(solution)/shard_map/reduce_scatter | solution.py:251
  886.2 534.1 %reduce-scatter.21.cloned.1.call-start = ((), (), s32[]{:S(2)}) async-start(), calls=%async_computation.20 | async-start | bytes 2228224 | tf_op jit(solution)/shard_map/reduce_scatter | solution.py:247
  893.1 592.1 %reduce-scatter.23.cloned.1.call-start = ((), (), s32[]{:S(2)}) async-start(), calls=%async_computation.21 | async-start | bytes 2228224 | tf_op jit(solution)/shard_map/reduce_scatter | solution.py:248
  899.8 650.6 %reduce-scatter.25.cloned.1.call-start = ((), (), s32[]{:S(2)}) async-start(), calls=%async_computation.22 | async-start | bytes 2228224 | tf_op jit(solution)/shard_map/reduce_scatter | solution.py:249
  906.4 25.4 %copy-start.26 = (f32[1024]{0:T(1024)S(1)}, f32[1024]{0:T(1024)}, u32[]{:S(2)}) copy-start(f32[1024]{0:T(1024)} %copy-done.25) | copy-start | bytes 12292
  906.4 708.7 %reduce-scatter.27.cloned.1.call-start = ((), (), s32[]{:S(2)}) async-start(), calls=%async_computation.23 | async-start | bytes 2228224 | tf_op jit(solution)/shard_map/reduce_scatter | solution.py:250
  913.4 120.1 %copy-start.24 = (f32[1024]{0:T(1024)S(1)}, f32[1024]{0:T(1024)}, u32[]{:S(2)}) copy-start(f32[1024]{0:T(1024)} %copy-done.23) | copy-start | bytes 12292
  913.4 120.1 %copy-start.28 = (f32[1024]{0:T(1024)S(1)}, f32[1024]{0:T(1024)}, u32[]{:S(2)}) copy-start(f32[1024]{0:T(1024)} %copy-done.27) | copy-start | bytes 12292
  (35 other events, 150.9 us)
Sparse Core Ops, SparseCore 0:
  13.5 59.4 all-gather.4
  205.0 99.2 reduce-scatter.12
  310.9 56.7 all-gather.6
  369.2 56.7 all-gather.8
  460.6 99.2 reduce-scatter.16
  570.8 56.7 all-gather.10
  832.5 99.2 reduce-scatter.18
  934.2 99.2 reduce-scatter.14
  1038.0 81.5 reduce-scatter.30
  1123.9 80.7 reduce-scatter.32
  1209.2 80.7 reduce-scatter.34
  1294.1 60.7 reduce-scatter.28
  1359.7 60.5 reduce-scatter.20
  1424.5 60.5 reduce-scatter.22
  1489.7 60.5 reduce-scatter.24
  1554.5 60.5 reduce-scatter.26
where the time goes:
time: 1630 us; the launch traced here: 1620 us
  waiting for transfers between devices  1090 us (67%)
  matrix products  343 us (21%)
  local copies, waits for them, and re-layouts  113 us (7%)
  other arithmetic  60.1 us (4%)
    reduce_scatter x1, waiting for transfers between devices, body(): lax.psum_scatter(jnp.dot(piece, out_weight, preferred_element_type=jnp.fl...  99.4 us
    reduce_scatter x1, waiting for transfers between devices, body(): lax.psum_scatter(total + jnp.einsum('rf,df->rd', right_low, right_weight,...  99.1 us
    reduce_scatter x1, waiting for transfers between devices, body(): lax.psum_scatter(jnp.dot(piece, down_weight, preferred_element_type=jnp.f...  98.1 us
    reduce_scatter x1, waiting for transfers between devices, body(): lax.psum_scatter(down_grad, 'dp', scatter_dimension=1, tiled=True)  85.2 us
    reduce_scatter x1, waiting for transfers between devices, body(): lax.psum_scatter(right_grad, 'dp', scatter_dimension=0, tiled=True)  85.1 us
    reduce_scatter x1, waiting for transfers between devices, body(): lax.psum_scatter(left_grad, 'dp', scatter_dimension=0, tiled=True)  74.9 us
    reduce_scatter x1, waiting for transfers between devices, body(): lax.psum_scatter(query_wgrad, 'dp', scatter_dimension=0, tiled=True)  65.4 us
    reduce_scatter x1, waiting for transfers between devices, body(): lax.psum_scatter(value_wgrad, 'dp', scatter_dimension=0, tiled=True)  65.2 us
  transfers between devices with their start and end apart: 16, of which 16 were waited for; matrix products, arithmetic and copies ran while one was open for 8% of the time, Pallas kernels for 0%

commit v1 on v0

v1 whole, which is shorter than its diff:
```python
import jax
import jax.numpy as jnp
from jax import lax
from jax.sharding import PartitionSpec as P

HEADS = 16
HEAD_DIM = 64
SEQ_LEN = 2048
CHUNK = 256
EPS = 1e-06
AXES = ("dp", "tensor")
LOW = jnp.bfloat16
F32 = jnp.float32


def mm(a, b, dims, out=F32):
    return lax.dot_general(a, b, ((dims[0], dims[1]), ((), ())), preferred_element_type=F32).astype(out)


def nn(a, b):
    return mm(a, b, ((1,), (0,)))


def nt_(a, b):
    return mm(a, b, ((1,), (1,)))


def norm_rows(values):
    factor = lax.rsqrt(jnp.mean(values * values, axis=-1, keepdims=True) + EPS)
    return (values * factor, factor)


def norm_back(grad_rows, normed, factor):
    return factor * (grad_rows - normed * jnp.mean(grad_rows * normed, axis=-1, keepdims=True))


class Comm:
    def __init__(self):
        self.nt = lax.axis_size("tensor")
        self.nd = lax.axis_size("dp")
        self.t = lax.axis_index("tensor")
        self.d = lax.axis_index("dp")
        self.core = self.d % 2
        self.y = (self.d // 2) % 2
        self.bits = self.nd.bit_length() - 1

    def send(self, values, partner):
        pairs = []
        for d in range(self.nd):
            for t in range(self.nt):
                d2, t2 = partner(d, t)
                pairs.append((d * self.nt + t, d2 * self.nt + t2))
        return lax.ppermute(values, AXES, pairs)

    def over_x(self, values):
        return self.send(values, lambda d, t: (d, t ^ 1))

    def over_bit(self, values, bit):
        return self.send(values, lambda d, t: (d ^ (1 << bit), t))

    def first(self, values):
        return self.send(values, lambda d, t: (d ^ 2, t) if d & 1 else (d, t ^ 1))

    def second(self, values):
        return self.send(values, lambda d, t: (d, t ^ 1) if d & 1 else (d ^ 2, t))


def piece_rows(rows):
    shared = (6 * rows // 32 + 8) // 16 * 16
    return (rows - 2 * shared) // 4, shared


def fetch_other(c, arrays):
    one, two = [], []
    for a in arrays:
        p, s = piece_rows(a.shape[0])
        one.append(lax.dynamic_slice_in_dim(a, (2 * c.y + c.core) * p, p, 0))
        two.append(lax.dynamic_slice_in_dim(a, 4 * p + c.core * s, s, 0))
    one = c.over_x(jnp.concatenate(one, 0))
    two = c.over_x(jnp.concatenate(two, 0))
    one_y = c.over_bit(one, 1)
    one_c, one_yc, two_c = (c.over_bit(v, 0) for v in (one, one_y, two))
    outs = []
    at_p = at_s = 0
    for a in arrays:
        p, s = piece_rows(a.shape[0])
        full = jnp.zeros(a.shape, a.dtype)
        for block, yy, cc in (
            (one, c.y, c.core),
            (one_y, 1 - c.y, c.core),
            (one_c, c.y, 1 - c.core),
            (one_yc, 1 - c.y, 1 - c.core),
        ):
            full = lax.dynamic_update_slice_in_dim(full, block[at_p : at_p + p], (2 * yy + cc) * p, 0)
        for block, cc in ((two, c.core), (two_c, 1 - c.core)):
            full = lax.dynamic_update_slice_in_dim(full, block[at_s : at_s + s], 4 * p + cc * s, 0)
        at_p += p
        at_s += s
        outs.append(full)
    return outs


def relative_rows(c, values):
    rows, width = values.shape
    k = c.bits
    x = values.T.reshape((2,) * k + (width // c.nd, rows))
    for axis in range(k):
        bit = (c.d >> (k - 1 - axis)) % 2
        x = jnp.where(bit == 1, jnp.flip(x, axis), x)
    x = jnp.transpose(x, tuple(reversed(range(k))) + (k, k + 1))
    return x.reshape(width, rows)


def add(a, b, out=LOW):
    return (a.astype(F32) + b.astype(F32)).astype(out)


def reduce_grads(c, own, other):
    half = own.shape[0] // 2
    own_r = c.over_bit(own[half:], 0)
    other_r = c.over_bit(other[half:], 0)
    a0 = add(own[:half], own_r)
    a1 = add(other[:half], other_r)
    q = half // 2
    is0 = c.core == 0
    keep0, keep1 = a0[:q], jnp.where(is0, a0[q:], a1[:q])
    away = jnp.concatenate([jnp.where(is0, a1[:q], a0[q:]), a1[q:]], 0)
    got = c.first(away)
    b0, b1 = add(keep0, got[:q]), add(keep1, got[q:])
    total = add(b0, c.second(b1), F32 if c.bits == 2 else LOW)
    for bit in range(2, c.bits):
        h = total.shape[0] // 2
        total = add(total[:h], c.over_bit(total[h:], bit), F32 if bit == c.bits - 1 else LOW)
    return total


def split_chunks(v):
    rows, width = v.shape
    ch = min(CHUNK, rows)
    return v.reshape(rows // ch, ch, width // HEAD_DIM, HEAD_DIM)


def merge_chunks(v):
    return v.reshape(v.shape[0] * v.shape[1], -1)


def causal(n):
    return (lax.broadcasted_iota(jnp.int32, (n, n), 0) >= lax.broadcasted_iota(jnp.int32, (n, n), 1)).astype(F32)


def ein(spec, a, b):
    return jnp.einsum(spec, a, b, preferred_element_type=F32)


def exclusive(sums, reverse=False):
    run = jnp.cumsum(sums[::-1] if reverse else sums, axis=0)
    run = run[::-1] if reverse else run
    return run - sums


def attend_local(q, k, v):
    q, k, v = split_chunks(q), split_chunks(k), split_chunks(v)
    w = (ein("nqhe,nkhe->nhqk", q, k) * causal(q.shape[1])).astype(LOW)
    inside = ein("nhqk,nkhe->nqhe", w, v)
    sums = ein("nkhe,nkhf->nhef", k, v)
    states = exclusive(sums)
    carried = ein("nqhe,nhef->nqhf", q, states.astype(LOW))
    return merge_chunks(inside + carried), states, jnp.sum(sums, 0)


def attend_back(q, k, v, g, states, later):
    q, k, v, g = (split_chunks(a) for a in (q, k, v, g))
    mask = causal(q.shape[1])
    w = (ein("nqhe,nkhe->nhqk", q, k) * mask).astype(LOW)
    p = (ein("nqhe,nkhe->nhqk", g, v) * mask).astype(LOW)
    sums = ein("nqhe,nqhf->nhef", q, g)
    after = (exclusive(sums, True) + later).astype(LOW)
    states = states.astype(LOW)
    dq = ein("nhqk,nkhe->nqhe", p, k) + ein("nqhf,nhef->nqhe", g, states)
    dk = ein("nhqk,nqhe->nkhe", p, q) + ein("nkhf,nhef->nkhe", v, after)
    dv = ein("nhqk,nqhe->nkhe", w, g) + ein("nkhe,nhef->nkhf", k, after)
    return merge_chunks(dq), merge_chunks(dk), merge_chunks(dv)


def other_sums(c, sums, earlier):
    if c.nt == 2:
        got = c.over_x(sums.astype(LOW)).astype(F32)
        h = got.shape[0] // 2
        got = jnp.concatenate([got[h:], got[:h]], 0)
        return jnp.where(c.t == (1 if earlier else 0), got, 0.0)
    every = lax.all_gather(sums.astype(LOW), "tensor", axis=0).astype(F32)
    ids = lax.broadcasted_iota(jnp.int32, every.shape, 0)
    return jnp.sum(jnp.where(ids < c.t if earlier else ids > c.t, every, 0.0), axis=0)


def body(tokens, qw, kw, vw, gw, ow, lw, rw, dw, cot):
    c = Comm()
    rows = tokens.shape[0]
    if c.nt == 2:
        attn_w = [[qw, kw, vw, gw], fetch_other(c, [qw, kw, vw, gw])]
        ow2, dw2 = fetch_other(c, [ow, dw])
        lw2, rw2 = fetch_other(c, [lw, rw])
        out_w = [ow, ow2]
        ffn_w = [(lw, rw, dw), (lw2, rw2, dw2)]
    else:
        cols = lambda a: lax.all_gather(a, "tensor", axis=1, tiled=True)
        attn_w = [[cols(a) for a in (qw, kw, vw, gw)]]
        out_w = [lax.all_gather(ow, "tensor", axis=0, tiled=True)]
        ffn_w = [(cols(lw), cols(rw), lax.all_gather(dw, "tensor", axis=0, tiled=True))]
    parts = range(len(attn_w))

    inputs = tokens.astype(F32)
    normed_in, norm_in = norm_rows(inputs)
    low_in = normed_in.astype(LOW)
    low_in_t = relative_rows(c, low_in)
    cot_t = relative_rows(c, cot)

    q, k, v, gate, sq, sk, attn, states, sums = ([] for _ in range(9))
    for i in parts:
        w = attn_w[i]
        qp, kp = nn(low_in, w[0]), nn(low_in, w[1])
        q.append(jax.nn.softplus(qp).astype(LOW))
        k.append(jax.nn.softplus(kp).astype(LOW))
        sq.append(jax.nn.sigmoid(qp).astype(LOW))
        sk.append(jax.nn.sigmoid(kp).astype(LOW))
        v.append(nn(low_in, w[2]).astype(LOW))
        gate.append(nn(low_in, w[3]).astype(LOW))
        a, st, su = attend_local(q[i], k[i], v[i])
        attn.append(a)
        states.append(st)
        sums.append(su)
    before = other_sums(c, jnp.concatenate(sums, 0), True)
    branch = 0.0
    heads_each = HEADS // len(attn_w)
    normed, factor, mixed = [], [], []
    for i in parts:
        pre = before[i * heads_each : (i + 1) * heads_each]
        states[i] = states[i] + pre
        a = attn[i].reshape(rows, heads_each, HEAD_DIM)
        a = a + ein("qhe,hef->qhf", q[i].reshape(a.shape), pre.astype(LOW))
        ms = jnp.mean(a * a, axis=-1, keepdims=True)
        r = lax.rsqrt(jnp.maximum(ms, 1.0))
        factor.append((r, (ms > 1.0).astype(F32)))
        n = a * r
        normed.append(n)
        m = (n.reshape(rows, -1) * gate[i]).astype(LOW)
        mixed.append(m)
        branch = branch + nn(m, out_w[i])
    residual = inputs + branch
    normed_mid, norm_mid = norm_rows(residual)
    low_mid = normed_mid.astype(LOW)
    low_mid_t = relative_rows(c, low_mid)

    ffn_out = mid_grad = 0.0
    ffn_grads = []
    for i in parts:
        lwi, rwi, dwi = ffn_w[i]
        left, right = nn(low_mid, lwi), nn(low_mid, rwi)
        prod = (left * right).astype(LOW)
        ffn_out = ffn_out + nn(prod, dwi)
        pg = nt_(cot, dwi)
        ll, rl = (pg * right).astype(LOW), (pg * left).astype(LOW)
        mid_grad = mid_grad + nt_(ll, lwi) + nt_(rl, rwi)
        ffn_grads.append(tuple(mm(a, b, ((1,), (0,)), LOW) for a, b in ((cot_t, prod), (low_mid_t, ll), (low_mid_t, rl))))
    result = (residual + ffn_out).astype(LOW)
    resid_grad = cot.astype(F32) + norm_back(mid_grad, normed_mid, norm_mid)
    low_resid = resid_grad.astype(LOW)
    low_resid_t = relative_rows(c, low_resid)

    gate_low, attn_low, sums, out_grads, gate_grads = [], [], [], [], []
    for i in parts:
        mg = nt_(low_resid, out_w[i])
        shape = (rows, heads_each, HEAD_DIM)
        n = normed[i]
        gate_low.append((mg * n.reshape(rows, -1)).astype(LOW))
        m = (mg * gate[i]).reshape(shape)
        r, above = factor[i]
        al = (r * (m - above * n * jnp.mean(m * n, axis=-1, keepdims=True))).astype(LOW)
        attn_low.append(al.reshape(rows, -1))
        sums.append(ein("qhe,qhf->hef", q[i].reshape(shape), al))
        out_grads.append(mm(low_resid_t, mixed[i], ((1,), (0,)), LOW))
        gate_grads.append(mm(low_in_t, gate_low[i], ((1,), (0,)), LOW))
    later = other_sums(c, jnp.concatenate(sums, 0), False)
    in_grad = 0.0
    qkv_grads = []
    for i in parts:
        lat = later[i * heads_each : (i + 1) * heads_each]
        dq, dk, dv = attend_back(q[i], k[i], v[i], attn_low[i], states[i], lat)
        dq, dk, dv = (dq * sq[i]).astype(LOW), (dk * sk[i]).astype(LOW), dv.astype(LOW)
        qkv_grads.append(tuple(mm(low_in_t, d, ((1,), (0,)), LOW) for d in (dq, dk, dv)))
        for d, w in zip((dq, dk, dv, gate_low[i]), attn_w[i]):
            in_grad = in_grad + nt_(d, w)
    tokens_grad = resid_grad + norm_back(in_grad, normed_in, norm_in)

    if c.nt == 2:

        def reduced(groups):
            own, other = (jnp.concatenate(g, 1) for g in groups)
            total = reduce_grads(c, own, other)
            width = total.shape[1] // len(groups[0])
            return [total[:, j * width : (j + 1) * width] for j in range(len(groups[0]))]

    else:

        def reduced(groups):
            outs = []
            for g in groups[0]:
                width = g.shape[1] // c.nt
                x = lax.psum_scatter(g, "tensor", scatter_dimension=1, tiled=True)
                k_ = c.bits
                x = x.reshape((2,) * k_ + (x.shape[0] // c.nd, width))
                x = jnp.transpose(x, tuple(reversed(range(k_))) + (k_, k_ + 1))
                for axis in range(k_):
                    bit = (c.d >> (k_ - 1 - axis)) % 2
                    x = jnp.where(bit == 1, jnp.flip(x, axis), x)
                x = x.reshape(-1, width)
                outs.append(lax.psum_scatter(x, "dp", scatter_dimension=0, tiled=True).astype(F32))
            return outs

    down_g, left_g, right_g = reduced(ffn_grads)
    out_g, gate_g = reduced([(a, b) for a, b in zip(out_grads, gate_grads)])
    q_g, k_g, v_g = reduced(qkv_grads)
    return (result, tokens_grad, q_g, k_g, v_g, gate_g, out_g.T, left_g, right_g, down_g.T)


def solution(mesh):
    rows, cols = P(AXES, None), P(None, "tensor")
    lead = P("tensor", None)
    return jax.shard_map(
        body,
        mesh=mesh,
        in_specs=(rows, cols, cols, cols, cols, lead, cols, cols, lead, rows),
        out_specs=(
            rows,
            rows,
            P("dp", "tensor"),
            P("dp", "tensor"),
            P("dp", "tensor"),
            P("dp", "tensor"),
            P("tensor", "dp"),
            P("dp", "tensor"),
            P("dp", "tensor"),
            P("tensor", "dp"),
        ),
        check_vma=False,
    )
```

time: 1630 us -> 676 us (0.41)
  waiting for transfers between devices: 1090 us -> 153 us
  matrix products: 343 us -> 220 us
  local copies, waits for them, and re-layouts: 113 us -> 154 us
  other arithmetic: 60.1 us -> 98.4 us
  starting transfers between devices: 1.42 us -> 34.8 us
    reduce_scatter x12 -> x0, waiting for transfers between devices: 885 us -> none  [the longest x1 99.4 us: body(): lax.psum_scatter(jnp.dot(piece, out_weight, preferred_element_type=jnp.fl...]
    all_gather x4 -> x0, waiting for transfers between devices: 202 us -> none  [the longest x1 59.5 us: body(): normed_all = lax.all_gather(normed_low, 'tensor', axis=0, tiled=True)]
    ppermute x0 -> x38, waiting for transfers between devices: none -> 153 us  [send(): return lax.ppermute(values, AXES, pairs)]
    dot_general x68 -> x76, matrix products: 343 us -> 220 us  [the longest x48 179 us: mm(): lax.dot_general(a, b, ((dims[0], dims[1]), ((), ())), preferred_element_t...]
    another operation x12 -> x8, local copies, waits for them, and re-layouts: 65.9 us -> 4.22 us  [the longest x2 3.52 us: body(): a = attn[i].reshape(rows, heads_each, HEAD_DIM)]
    ppermute x0 -> x38, starting transfers between devices: none -> 34.8 us  [send(): return lax.ppermute(values, AXES, pairs)]
    unnamed x76 -> x359, local copies, waits for them, and re-layouts: 31.1 us -> 62.5 us
    reshape x0 -> x12, local copies, waits for them, and re-layouts: none -> 31.1 us  [the longest x8 24.4 us: split_chunks(): return v.reshape(rows // ch, ch, width // HEAD_DIM, HEAD_DIM)]
  transfers between devices with their start and end apart: 16 -> 38, of which waited for: 16 -> 11; matrix products, arithmetic and copies ran while one was open for 8% -> 65% of each run, Pallas kernels for 0% -> 0%
where the time goes in v1:
time: 676 us; the launch traced here: 664 us
  matrix products  220 us (33%)
  local copies, waits for them, and re-layouts  154 us (23%)
  waiting for transfers between devices  153 us (23%)
  other arithmetic  98.4 us (15%)
  starting transfers between devices  34.8 us (5%)
    dot_general x48, matrix products, mm(): lax.dot_general(a, b, ((dims[0], dims[1]), ((), ())), preferred_element_t...  179 us
    ppermute x38, waiting for transfers between devices, send(): return lax.ppermute(values, AXES, pairs)  153 us
    unnamed x359, local copies, waits for them, and re-layouts  62.5 us
    dot_general x28, matrix products, ein(): return jnp.einsum(spec, a, b, preferred_element_type=F32)  41 us
    ppermute x38, starting transfers between devices, send(): return lax.ppermute(values, AXES, pairs)  34.8 us
    convert_element_type x15, other arithmetic, add(): return (a.astype(F32) + b.astype(F32)).astype(out)  31.9 us
    reshape x8, local copies, waits for them, and re-layouts, split_chunks(): return v.reshape(rows // ch, ch, width // HEAD_DIM, HEAD_DIM)  24.4 us
    select_n x15, other arithmetic, relative_rows(): x = jnp.where(bit == 1, jnp.flip(x, axis), x)  20.5 us
  transfers between devices with their start and end apart: 38, of which 11 were waited for; matrix products, arithmetic and copies ran while one was open for 65% of the time, Pallas kernels for 0%

profile of v1, /device:TPU:0, one launch (start us, length us, event | category | flops | bytes accessed | tf_op | source)
XLA Modules:
  0.0 664.2 jit_solution(8700550580961664086)
XLA Ops:
  67.4 5.6 reverse_select_fusion.7
  103.4 5.5 collective-permute-done.8
  111.2 15.6 %collective-permute-done.1 = bf16[640,512]{1,0:T(8,128)(2,1)S(1)} collective-permute-done((bf16[640,512]{1,0:T(8,128)(2,1)}, bf16[640,512]{1,0:T(8,128)(2,1)S(1)}, u32[]{:S(2)}, u32[]{:S(2)}) %collective-permute-start.1) | collective-permute-done | bytes 655392 | tf_op jit(solution)/shard_map/ppermute | solution.py:53
  128.0 14.8 %collective-permute-done.14 = bf16[320,1408]{1,0:T(8,128)(2,1)} collective-permute-done((bf16[320,1408]{1,0:T(8,128)(2,1)}, bf16[320,1408]{1,0:T(8,128)(2,1)}, u32[]{:S(2)}, u32[]{:S(2)}) %collective-permute-start.14) | collective-permute-done | bytes 901152 | tf_op jit(solution)/shard_map/ppermute | solution.py:53
  148.0 5.6 fusion.92
  167.7 5.6 fusion.14
  181.3 5.6 fusion.15
  224.3 5.9 multiply_convert_fusion.4
  230.3 7.1 %fusion.88 = f32[1024,1024]{0,1:T(8,128)} fusion(bf16[1024,1408]{1,0:T(8,128)(2,1)} %get-tuple-element.45, bf16[1408,1024]{1,0:T(8,128)(2,1)S(1)} %copy-done), kind=kOutput, calls=%fused_computation.312 | convolution fusion | flops 2952790016 | bytes 9961472 | tf_op jit(solution)/shard_map/dot_general | solution.py:17
  237.4 5.0 fusion.90
  260.2 5.0 fusion.91
  280.8 6.0 fusion.3
  286.8 8.2 %fusion.93 = f32[1024,1024]{0,1:T(8,128)} fusion(bf16[1024,1408]{1,0:T(8,128)(2,1)} %get-tuple-element.47, bf16[1024,1408]{1,0:T(8,128)(2,1)} %copy-done.108), kind=kOutput, calls=%fused_computation.317 | convolution fusion | flops 2952790016 | bytes 9961472 | tf_op jit(solution)/shard_map/dot_general | solution.py:17
  295.1 6.2 multiply_reduce_fusion
  382.1 4.8 add_convert_fusion.5
  458.0 6.2 add_convert_fusion.1
  472.0 13.0 %fusion.5 = (f32[1024]{0:T(1024)S(1)}, f32[1024,1024]{0,1:T(8,128)}) fusion(bf16[1024,1024]{0,1:T(8,128)(2,1)S(1)} %copy-done.7, f32[1024]{0:T(1024)S(1)} %copy-done.158, f32[1024,1024]{0,1:T(8,128)} %fusion.100, f32[1024,1024]{0,1:T(8,128)} %fusion.99, f32[1024,1024]{0,1:T(8,128)} %fusion.98, f32[1024,1024]{0,1:T(8,128)} %fusion.97, ...), kind=kOutput, calls=%fused_computation.30 | convolution fusion | flops 1085275136 | bytes 37756928 | tf_op jit(solution)/shard_map/dot_general | solution.py:17
  495.5 35.9 %collective-permute-done.28 = bf16[512,1024]{0,1:T(8,128)(2,1)S(1)} collective-permute-done((bf16[512,1024]{0,1:T(8,128)(2,1)S(1)}, bf16[512,1024]{0,1:T(8,128)(2,1)S(1)}, u32[]{:S(2)}, u32[]{:S(2)}) %collective-permute-start.28) | collective-permute-done | bytes 1048608 | tf_op jit(solution)/shard_map/ppermute | solution.py:53
  542.8 6.0 fusion.8
  548.8 5.5 copy.258
  557.1 19.4 %collective-permute-done.22 = bf16[512,1536]{0,1:T(8,128)(2,1)} collective-permute-done((bf16[512,1536]{0,1:T(8,128)(2,1)}, bf16[512,1536]{0,1:T(8,128)(2,1)}, u32[]{:S(2)}, u32[]{:S(2)}) %collective-permute-start.22) | collective-permute-done | bytes 1572896 | tf_op jit(solution)/shard_map/ppermute | solution.py:53
  595.0 23.9 %collective-permute-done.24 = bf16[128,1536]{0,1:T(8,128)(2,1)} collective-permute-done((bf16[128,1536]{0,1:T(8,128)(2,1)S(1)}, bf16[128,1536]{0,1:T(8,128)(2,1)}, u32[]{:S(2)}, u32[]{:S(2)}) %collective-permute-start.24) | collective-permute-done | bytes 393248 | tf_op jit(solution)/shard_map/ppermute | solution.py:53
  625.7 25.4 %collective-permute-done.25 = bf16[64,1536]{0,1:T(8,128)(2,1)S(1)} collective-permute-done((bf16[64,1536]{0,1:T(8,128)(2,1)S(1)}, bf16[64,1536]{0,1:T(8,128)(2,1)S(1)}, u32[]{:S(2)}, u32[]{:S(2)}) %collective-permute-start.25) | collective-permute-done | bytes 196640 | tf_op jit(solution)/shard_map/ppermute | solution.py:53
  653.6 8.1 %collective-permute-done.37 = bf16[64,4224]{1,0:T(8,128)(2,1)} collective-permute-done((bf16[64,4224]{1,0:T(8,128)(2,1)}, bf16[64,4224]{1,0:T(8,128)(2,1)}, u32[]{:S(2)}, u32[]{:S(2)}) %collective-permute-start.37) | collective-permute-done | bytes 540704 | tf_op jit(solution)/shard_map/ppermute | solution.py:53
  (669 shorter events, 410.9 us)
Async XLA Ops:
  3.8 90.7 %collective-permute-start = (bf16[640,512]{1,0:T(8,128)(2,1)}, bf16[640,512]{1,0:T(8,128)(2,1)}, u32[]{:S(2)}, u32[]{:S(2)}) collective-permute-start(bf16[640,512]{1,0:T(8,128)(2,1)} %pad_maximum_fusion.13), channel_id=1, source_target_pairs={{0,1},{1,0},{2,3},{3,2},{4,5},{5,4},{6,7},{7,6},{8,9},{9,8},{10,11... | collective-permute-start | bytes 1966088 | tf_op jit(solution)/shard_map/ppermute | solution.py:53
  9.8 117.0 %collective-permute-start.4 = (bf16[768,512]{1,0:T(8,128)(2,1)}, bf16[768,512]{1,0:T(8,128)(2,1)}, u32[]{:S(2)}, u32[]{:S(2)}) collective-permute-start(bf16[768,512]{1,0:T(8,128)(2,1)} %pad_maximum_fusion.11), channel_id=1, source_target_pairs={{0,1},{1,0},{2,3},{3,2},{4,5},{5,4},{6,7},{7,6},{8,9},{9,8},{10,11... | collective-permute-start | bytes 2359304 | tf_op jit(solution)/shard_map/ppermute | solution.py:53
  11.7 80.3 %collective-permute-start.7 = (bf16[296,1024]{1,0:T(8,128)(2,1)}, bf16[296,1024]{1,0:T(8,128)(2,1)}, u32[]{:S(2)}, u32[]{:S(2)}) collective-permute-start(bf16[296,1024]{1,0:T(8,128)(2,1)} %pad_maximum_fusion.14), channel_id=1, source_target_pairs={{0,1},{1,0},{2,3},{3,2},{4,5},{5,4},{6,7},{7,6},{8,9},{9,8},{10,11... | collective-permute-start | bytes 1818632 | tf_op jit(solution)/shard_map/ppermute | solution.py:53
  15.7 95.0 %collective-permute-start.11 = (bf16[368,1024]{1,0:T(8,128)(2,1)}, bf16[368,1024]{1,0:T(8,128)(2,1)}, u32[]{:S(2)}, u32[]{:S(2)}) collective-permute-start(bf16[368,1024]{1,0:T(8,128)(2,1)} %pad_maximum_fusion.12), channel_id=1, source_target_pairs={{0,1},{1,0},{2,3},{3,2},{4,5},{5,4},{6,7},{7,6},{8,9},{9,8},{10,11... | collective-permute-start | bytes 2261000 | tf_op jit(solution)/shard_map/ppermute | solution.py:53
  17.9 82.8 %collective-permute-start.13 = (bf16[320,1408]{1,0:T(8,128)(2,1)}, bf16[320,1408]{1,0:T(8,128)(2,1)}, u32[]{:S(2)}, u32[]{:S(2)}) collective-permute-start(bf16[320,1408]{1,0:T(8,128)(2,1)} %pad_maximum_fusion.10), channel_id=1, source_target_pairs={{0,1},{1,0},{2,3},{3,2},{4,5},{5,4},{6,7},{7,6},{8,9},{9,8},{10,11... | collective-permute-start | bytes 2703368 | tf_op jit(solution)/shard_map/ppermute | solution.py:53
  92.0 35.4 %collective-permute-start.17 = (bf16[384,1408]{1,0:T(8,128)(2,1)S(1)}, bf16[384,1408]{1,0:T(8,128)(2,1)}, u32[]{:S(2)}, u32[]{:S(2)}) collective-permute-start(bf16[384,1408]{1,0:T(8,128)(2,1)S(1)} %pad_maximum_fusion.6), channel_id=1, source_target_pairs={{0,1},{1,0},{2,3},{3,2},{4,5},{5,4},{6,7},{7,6},{8,9},{9,8},{10,11... | collective-permute-start | bytes 3244040 | tf_op jit(solution)/shard_map/ppermute | solution.py:53
  110.8 32.0 %collective-permute-start.14 = (bf16[320,1408]{1,0:T(8,128)(2,1)}, bf16[320,1408]{1,0:T(8,128)(2,1)}, u32[]{:S(2)}, u32[]{:S(2)}) collective-permute-start(bf16[320,1408]{1,0:T(8,128)(2,1)} %collective-permute-done.13), channel_id=1, source_target_pairs={{0,4},{1,5},{2,6},{3,7},{4,0},{5,1},{6,2},{7,3},{8,12},{9,13},{10,... | collective-permute-start | bytes 2703368 | tf_op jit(solution)/shard_map/ppermute | solution.py:53
  127.4 29.1 %collective-permute-start.5 = (bf16[768,512]{1,0:T(8,128)(2,1)}, bf16[768,512]{1,0:T(8,128)(2,1)S(1)}, u32[]{:S(2)}, u32[]{:S(2)}) collective-permute-start(bf16[768,512]{1,0:T(8,128)(2,1)} %collective-permute-done.4), channel_id=1, source_target_pairs={{0,2},{1,3},{2,0},{3,1},{4,6},{5,7},{6,4},{7,5},{8,10},{9,11},{10,... | collective-permute-start | bytes 2359304 | tf_op jit(solution)/shard_map/ppermute | solution.py:53
  127.5 147.7 %collective-permute-start.18 = (bf16[384,1408]{1,0:T(8,128)(2,1)}, bf16[384,1408]{1,0:T(8,128)(2,1)}, u32[]{:S(2)}, u32[]{:S(2)}) collective-permute-start(bf16[384,1408]{1,0:T(8,128)(2,1)} %collective-permute-done.17), channel_id=1, source_target_pairs={{0,2},{1,3},{2,0},{3,1},{4,6},{5,7},{6,4},{7,5},{8,10},{9,11},{10,... | collective-permute-start | bytes 3244040 | tf_op jit(solution)/shard_map/ppermute | solution.py:53
  144.8 127.6 %collective-permute-start.16 = (bf16[320,1408]{1,0:T(8,128)(2,1)}, bf16[320,1408]{1,0:T(8,128)(2,1)}, u32[]{:S(2)}, u32[]{:S(2)}) collective-permute-start(bf16[320,1408]{1,0:T(8,128)(2,1)} %collective-permute-done.14), channel_id=1, source_target_pairs={{0,2},{1,3},{2,0},{3,1},{4,6},{5,7},{6,4},{7,5},{8,10},{9,11},{10,... | collective-permute-start | bytes 2703368 | tf_op jit(solution)/shard_map/ppermute | solution.py:53
  272.4 185.4 %collective-permute-start.32 = (bf16[512,4224]{1,0:T(8,128)(2,1)}, bf16[512,4224]{1,0:T(8,128)(2,1)}, u32[]{:S(2)}, u32[]{:S(2)}) collective-permute-start(bf16[512,4224]{1,0:T(8,128)(2,1)} %slice.520), channel_id=1, source_target_pairs={{0,2},{1,3},{2,0},{3,1},{4,6},{5,7},{6,4},{7,5},{8,10},{9,11},{10,... | collective-permute-start | bytes 12976136 | tf_op jit(solution)/shard_map/ppermute | solution.py:53
  401.1 83.9 %collective-permute-start.26 = (bf16[512,1024]{0,1:T(8,128)(2,1)}, bf16[512,1024]{0,1:T(8,128)(2,1)}, u32[]{:S(2)}, u32[]{:S(2)}) collective-permute-start(bf16[512,1024]{0,1:T(8,128)(2,1)} %pad_maximum_fusion.8), channel_id=1, source_target_pairs={{0,2},{1,3},{2,0},{3,1},{4,6},{5,7},{6,4},{7,5},{8,10},{9,11},{10,... | collective-permute-start | bytes 3145736 | tf_op jit(solution)/shard_map/ppermute | solution.py:53
  404.0 82.9 %collective-permute-start.27 = (bf16[512,1024]{0,1:T(8,128)(2,1)}, bf16[512,1024]{0,1:T(8,128)(2,1)}, u32[]{:S(2)}, u32[]{:S(2)}) collective-permute-start(bf16[512,1024]{0,1:T(8,128)(2,1)} %pad_maximum_fusion.7), channel_id=1, source_target_pairs={{0,2},{1,3},{2,0},{3,1},{4,6},{5,7},{6,4},{7,5},{8,10},{9,11},{10,... | collective-permute-start | bytes 3145736 | tf_op jit(solution)/shard_map/ppermute | solution.py:53
  411.4 52.8 %collective-permute-start.33 = (bf16[512,4224]{1,0:T(8,128)(2,1)}, bf16[512,4224]{1,0:T(8,128)(2,1)}, u32[]{:S(2)}, u32[]{:S(2)}) collective-permute-start(bf16[512,4224]{1,0:T(8,128)(2,1)} %slice.523), channel_id=1, source_target_pairs={{0,2},{1,3},{2,0},{3,1},{4,6},{5,7},{6,4},{7,5},{8,10},{9,11},{10,... | collective-permute-start | bytes 12976136 | tf_op jit(solution)/shard_map/ppermute | solution.py:53
  433.2 57.0 %collective-permute-start.20 = (bf16[512,1536]{0,1:T(8,128)(2,1)}, bf16[512,1536]{0,1:T(8,128)(2,1)}, u32[]{:S(2)}, u32[]{:S(2)}) collective-permute-start(bf16[512,1536]{0,1:T(8,128)(2,1)} %slice.487), channel_id=1, source_target_pairs={{0,2},{1,3},{2,0},{3,1},{4,6},{5,7},{6,4},{7,5},{8,10},{9,11},{10,... | collective-permute-start | bytes 4718600 | tf_op jit(solution)/shard_map/ppermute | solution.py:53
  457.8 34.8 %collective-permute-start.21 = (bf16[512,1536]{0,1:T(8,128)(2,1)}, bf16[512,1536]{0,1:T(8,128)(2,1)}, u32[]{:S(2)}, u32[]{:S(2)}) collective-permute-start(bf16[512,1536]{0,1:T(8,128)(2,1)} %slice.490), channel_id=1, source_target_pairs={{0,2},{1,3},{2,0},{3,1},{4,6},{5,7},{6,4},{7,5},{8,10},{9,11},{10,... | collective-permute-start | bytes 4718600 | tf_op jit(solution)/shard_map/ppermute | solution.py:53
  470.1 63.0 %collective-permute-start.34 = (bf16[512,4224]{1,0:T(8,128)(2,1)S(1)}, bf16[512,4224]{1,0:T(8,128)(2,1)}, u32[]{:S(2)}, u32[]{:S(2)}) collective-permute-start(bf16[512,4224]{1,0:T(8,128)(2,1)S(1)} %pad_maximum_fusion.2), channel_id=1, source_target_pairs={{0,1},{1,0},{2,6},{3,7},{4,5},{5,4},{6,2},{7,3},{8,9},{9,8},{10,14... | collective-permute-start | bytes 12976136 | tf_op jit(solution)/shard_map/ppermute | solution.py:53
  488.7 42.6 %collective-permute-start.28 = (bf16[512,1024]{0,1:T(8,128)(2,1)S(1)}, bf16[512,1024]{0,1:T(8,128)(2,1)S(1)}, u32[]{:S(2)}, u32[]{:S(2)}) collective-permute-start(bf16[512,1024]{0,1:T(8,128)(2,1)S(1)} %pad_maximum_fusion.9), channel_id=1, source_target_pairs={{0,1},{1,0},{2,6},{3,7},{4,5},{5,4},{6,2},{7,3},{8,9},{9,8},{10,14... | collective-permute-start | bytes 3145736 | tf_op jit(solution)/shard_map/ppermute | solution.py:53
  537.0 43.9 %collective-permute-start.35 = (bf16[256,4224]{1,0:T(8,128)(2,1)}, bf16[256,4224]{1,0:T(8,128)(2,1)}, u32[]{:S(2)}, u32[]{:S(2)}) collective-permute-start(bf16[256,4224]{1,0:T(8,128)(2,1)} %add_convert_fusion.3), channel_id=1, source_target_pairs={{0,4},{1,5},{2,3},{3,2},{4,0},{5,1},{6,7},{7,6},{8,12},{9,13},{10,... | collective-permute-start | bytes 6488072 | tf_op jit(solution)/shard_map/ppermute | solution.py:53
  538.9 37.6 %collective-permute-start.22 = (bf16[512,1536]{0,1:T(8,128)(2,1)}, bf16[512,1536]{0,1:T(8,128)(2,1)}, u32[]{:S(2)}, u32[]{:S(2)}) collective-permute-start(bf16[512,1536]{0,1:T(8,128)(2,1)} %pad_maximum_fusion.5), channel_id=1, source_target_pairs={{0,1},{1,0},{2,6},{3,7},{4,5},{5,4},{6,2},{7,3},{8,9},{9,8},{10,14... | collective-permute-start | bytes 4718600 | tf_op jit(solution)/shard_map/ppermute | solution.py:53
  554.5 38.8 %collective-permute-start.31 = (bf16[64,1024]{0,1:T(8,128)(2,1)S(1)}, bf16[64,1024]{0,1:T(8,128)(2,1)S(1)}, u32[]{:S(2)}, u32[]{:S(2)}) collective-permute-start(bf16[64,1024]{0,1:T(8,128)(2,1)S(1)} %slice.516), channel_id=1, source_target_pairs={{0,16},{1,17},{2,18},{3,19},{4,20},{5,21},{6,22},{7,23},{8,24},{9,... | collective-permute-start | bytes 393224 | tf_op jit(solution)/shard_map/ppermute | solution.py:53
  585.8 37.1 %collective-permute-start.36 = (bf16[128,4224]{1,0:T(8,128)(2,1)}, bf16[128,4224]{1,0:T(8,128)(2,1)}, u32[]{:S(2)}, u32[]{:S(2)}) collective-permute-start(bf16[128,4224]{1,0:T(8,128)(2,1)} %slice.530), channel_id=1, source_target_pairs={{0,8},{1,9},{2,10},{3,11},{4,12},{5,13},{6,14},{7,15},{8,0},{9,1},... | collective-permute-start | bytes 3244040 | tf_op jit(solution)/shard_map/ppermute | solution.py:53
  620.3 30.8 %collective-permute-start.25 = (bf16[64,1536]{0,1:T(8,128)(2,1)S(1)}, bf16[64,1536]{0,1:T(8,128)(2,1)S(1)}, u32[]{:S(2)}, u32[]{:S(2)}) collective-permute-start(bf16[64,1536]{0,1:T(8,128)(2,1)S(1)} %slice.499), channel_id=1, source_target_pairs={{0,16},{1,17},{2,18},{3,19},{4,20},{5,21},{6,22},{7,23},{8,24},{9,... | collective-permute-start | bytes 589832 | tf_op jit(solution)/shard_map/ppermute | solution.py:53
  625.3 36.4 %collective-permute-start.37 = (bf16[64,4224]{1,0:T(8,128)(2,1)}, bf16[64,4224]{1,0:T(8,128)(2,1)}, u32[]{:S(2)}, u32[]{:S(2)}) collective-permute-start(bf16[64,4224]{1,0:T(8,128)(2,1)} %slice.532), channel_id=1, source_target_pairs={{0,16},{1,17},{2,18},{3,19},{4,20},{5,21},{6,22},{7,23},{8,24},{9,... | collective-permute-start | bytes 1622024 | tf_op jit(solution)/shard_map/ppermute | solution.py:53
  (186 other events, 1083.7 us)
